TPU v7x, 32 devices: a whole 2x2x4 slice. The times are simulated.
32 devices in a mesh: wide: 16 (over z, y, core), narrow: 2 (over x).
Axes of the slice: x: 2, y: 2, z: 4, core: 2. Of those that a mesh axis runs over, the one named last changes fastest.
Arguments:
- initial_warmth_state: float32 [128, 128, 256], P(None, 'wide', 'narrow'), may hold values from -1.5 to 1.5
- diffusivity_coefficient: float32 [128, 128, 256], P(None, 'wide', 'narrow'), may hold values from 0.5 to 8
- heating_supply: float32 [128, 128, 256], P(None, 'wide', 'narrow'), may hold values from -6 to 6
- known_forcing_vector: float32 [128, 128, 256], P(None, 'wide', 'narrow'), as said below
Outputs:
- advanced_warmth_state: float32 [128, 128, 256], P(None, 'wide', 'narrow')
- upcoming_forcing_vector: float32 [128, 128, 256], P(None, 'wide', 'narrow')
Inputs may be any that keep to these rules, and one draw needn't show every extreme that they name: `known_forcing_vector`: values lie within -6 to 6.
All inputs are finite; a program needn't handle non-finite values.
Results may differ from a plain program's by a relative error of at most 0.00035.
Values sent between devices are 32-bit elements; how exact they have to be, the bound alone decides.
A program may use at most 64 MiB of HBM per device.

v0:
```python
import jax
import jax.numpy as jnp
from jax import lax
from jax.sharding import PartitionSpec as P

HALF = 256


def extended(cells, sides, width):
    for axis, dim in sides:
        count = lax.axis_size(axis)
        ends = count - 1
        head = lax.slice_in_dim(cells, 0, width, axis=dim)
        tail = lax.slice_in_dim(cells, cells.shape[dim] - width, cells.shape[dim], axis=dim)
        cells = jnp.concatenate(
            [
                lax.ppermute(tail, axis, [(i, (i + 1) % count) for i in range(ends)]),
                cells,
                lax.ppermute(head, axis, [((i + 1) % count, i) for i in range(ends)]),
            ],
            axis=dim,
        )
    return cells


def solve_lines(below_band, main_band, above_band, right_side):
    length = right_side.shape[0]
    if length == 1:
        return right_side / main_band
    blank = jnp.zeros_like(right_side[:1])
    even_below = below_band[0::2]
    even_main = main_band[0::2]
    even_above = above_band[0::2]
    even_right = right_side[0::2]
    next_below = jnp.concatenate([even_below[1:], blank])
    next_main = jnp.concatenate([even_main[1:], blank + 1.0])
    next_above = jnp.concatenate([even_above[1:], blank])
    next_right = jnp.concatenate([even_right[1:], blank])
    factor_left = -below_band[1::2] / even_main
    factor_right = -above_band[1::2] / next_main
    reduced = solve_lines(
        factor_left * even_below,
        main_band[1::2] + factor_left * even_above + factor_right * next_below,
        factor_right * next_above,
        right_side[1::2] + factor_left * even_right + factor_right * next_right,
    )
    earlier = jnp.concatenate([blank, reduced[:-1]])
    solved_even = (even_right - even_below * earlier - even_above * reduced) / even_main
    return jnp.stack([solved_even, reduced], axis=1).reshape(right_side.shape)


def line_solve(cond, right_side):
    half_ratio = 1.0 * HALF
    blank = jnp.zeros_like(cond[:1])
    padded = jnp.concatenate([blank, cond, blank])
    face_low = 0.5 * (padded[:-2] + padded[1:-1])
    face_high = 0.5 * (padded[1:-1] + padded[2:])
    below_band = jnp.concatenate([blank, -half_ratio * face_low[1:]])
    above_band = jnp.concatenate([-half_ratio * face_high[:-1], blank])
    main_band = 1.0 + half_ratio * (face_low + face_high)
    return solve_lines(below_band, main_band, above_band, right_side)


def operator(padded):
    field = padded[0]
    cond = padded[1]
    centre = field[1:-1, 1:-1, 1:-1]
    middle = cond[1:-1, 1:-1, 1:-1]
    total = 0.5 * (middle + cond[:-2, 1:-1, 1:-1]) * (field[:-2, 1:-1, 1:-1] - centre)
    total = total + 0.5 * (middle + cond[2:, 1:-1, 1:-1]) * (field[2:, 1:-1, 1:-1] - centre)
    total = total + 0.5 * (middle + cond[1:-1, :-2, 1:-1]) * (field[1:-1, :-2, 1:-1] - centre)
    total = total + 0.5 * (middle + cond[1:-1, 2:, 1:-1]) * (field[1:-1, 2:, 1:-1] - centre)
    total = total + 0.5 * (middle + cond[1:-1, 1:-1, :-2]) * (field[1:-1, 1:-1, :-2] - centre)
    total = total + 0.5 * (middle + cond[1:-1, 1:-1, 2:]) * (field[1:-1, 1:-1, 2:] - centre)
    return total


def padded_pair(ghost_padded):
    return jnp.pad(ghost_padded, ((0, 0), (1, 1), (0, 0), (0, 0)))


def solve_second(pieces):
    values, conds = pieces
    return (line_solve(conds, values), conds)


def per_device(initial_warmth_state, diffusivity_coefficient, heating_supply, known_forcing_vector):
    time_ratio = 2.0 * HALF
    first = line_solve(diffusivity_coefficient, time_ratio * known_forcing_vector)
    second, cond_second = solve_second(
        (
            lax.all_to_all(
                jnp.swapaxes(first, 0, 1), "wide", split_axis=1, concat_axis=0, tiled=True
            ),
            lax.all_to_all(
                jnp.swapaxes(diffusivity_coefficient, 0, 1),
                "wide",
                split_axis=1,
                concat_axis=0,
                tiled=True,
            ),
        )
    )
    third_in, cond_third = (
        lax.all_to_all(second, "narrow", split_axis=0, concat_axis=2, tiled=True),
        lax.all_to_all(cond_second, "narrow", split_axis=0, concat_axis=2, tiled=True),
    )
    y_count, x_count, z_count = third_in.shape
    cond_lines = cond_third.reshape(y_count * x_count, z_count).T
    depthwise_pass = line_solve(cond_lines, third_in.reshape(y_count * x_count, z_count).T)
    third_block = depthwise_pass.T.reshape(y_count, x_count, z_count)
    flipped_array = lax.all_to_all(
        lax.all_to_all(third_block, "narrow", split_axis=2, concat_axis=0, tiled=True),
        "wide",
        split_axis=0,
        concat_axis=1,
        tiled=True,
    )
    advanced_warmth_state = initial_warmth_state + jnp.swapaxes(flipped_array, 0, 1)
    ghost_padded = extended(
        jnp.stack([advanced_warmth_state, diffusivity_coefficient]), (("wide", 2), ("narrow", 3)), 1
    )
    upcoming_forcing_vector = heating_supply + operator(padded_pair(ghost_padded))
    return (advanced_warmth_state, upcoming_forcing_vector)


def solution(mesh):
    placed = (
        P(None, "wide", "narrow"),
        P(None, "wide", "narrow"),
        P(None, "wide", "narrow"),
        P(None, "wide", "narrow"),
    )
    return jax.shard_map(
        per_device,
        mesh=mesh,
        in_specs=placed,
        out_specs=(P(None, "wide", "narrow"), P(None, "wide", "narrow")),
        check_vma=False,
    )
```

profile of v0, /device:TPU:1, one launch (start us, length us, event | category | flops | bytes accessed | tf_op | source)
XLA Modules:
  0.0 146.2 jit_solution(10686847486221317631)
XLA Ops:
  0.6 7.5 %all-to-all-start.1 = ((f32[8,128,128]{2,0,1:T(8,128)}), f32[8,128,128]{2,0,1:T(8,128)S(1)}, u32[]{:S(2)}, u32[]{:S(2)}) async-start(f32[8,128,128]{2,0,1:T(8,128)} %bitcast.159), calls=%async_computation.1 | async-start | bytes 1048576 | tf_op jit(solution)/shard_map/all_to_all | solution.py:95
  8.1 1.7 %multiply_add_fusion.2 = (f32[128,8,128]{2,1,0:T(8,128)S(1)}, f32[128,8,128]{2,1,0:T(8,128)S(1)}, f32[128,8,128]{2,1,0:T(8,128)S(1)}) fusion(f32[128,8,128]{2,1,0:T(8,128)} %param.5), kind=kLoop, calls=%fused_computation.71 | loop fusion | flops 917504 | bytes 2097152 | tf_op jit(solution)/shard_map/add | solution.py:60
  12.7 9.5 %all-to-all-done.1 = f32[8,128,128]{2,0,1:T(8,128)S(1)} async-done(((f32[8,128,128]{2,0,1:T(8,128)}), f32[8,128,128]{2,0,1:T(8,128)S(1)}, u32[]{:S(2)}, u32[]{:S(2)}) %all-to-all-start.1) | async-done | bytes 524320 | tf_op jit(solution)/shard_map/all_to_all | solution.py:95
  22.2 4.5 %all-to-all-start = ((f32[8,128,128]{2,0,1:T(8,128)}), f32[8,128,128]{2,0,1:T(8,128)S(1)}, u32[]{:S(2)}, u32[]{:S(2)}) async-start(f32[8,128,128]{2,0,1:T(8,128)} %bitcast.21), calls=%async_computation | async-start | bytes 1048576 | tf_op jit(solution)/shard_map/all_to_all | solution.py:92
  27.6 1.6 %multiply_add_fusion.1 = (f32[128,8,128]{2,1,0:T(8,128)S(1)}, f32[128,8,128]{2,1,0:T(8,128)S(1)}, f32[128,8,128]{2,1,0:T(8,128)S(1)}) fusion(f32[128,8,128]{2,1,0:T(8,128)} %bitcast.29), kind=kLoop, calls=%fused_computation.69 | loop fusion | flops 917504 | bytes 2097152 | tf_op jit(solution)/shard_map/add | solution.py:60
  29.5 11.3 %all-to-all-done = f32[8,128,128]{2,0,1:T(8,128)S(1)} async-done(((f32[8,128,128]{2,0,1:T(8,128)}), f32[8,128,128]{2,0,1:T(8,128)S(1)}, u32[]{:S(2)}, u32[]{:S(2)}) %all-to-all-start) | async-done | bytes 524320 | tf_op jit(solution)/shard_map/all_to_all | solution.py:92
  40.8 3.5 %all-to-all-start.3 = ((f32[128,8,128]{2,1,0:T(8,128)}), f32[128,8,128]{2,1,0:T(8,128)S(1)}, u32[]{:S(2)}, u32[]{:S(2)}) async-start(f32[128,8,128]{2,1,0:T(8,128)} %bitcast.29), calls=%async_computation.3 | async-start | bytes 1048576 | tf_op jit(solution)/shard_map/all_to_all | solution.py:106
  47.0 4.9 %all-to-all-done.3 = f32[128,8,128]{2,1,0:T(8,128)S(1)} async-done(((f32[128,8,128]{2,1,0:T(8,128)}), f32[128,8,128]{2,1,0:T(8,128)S(1)}, u32[]{:S(2)}, u32[]{:S(2)}) %all-to-all-start.3) | async-done | bytes 524320 | tf_op jit(solution)/shard_map/all_to_all | solution.py:106
  51.9 3.5 %all-to-all-start.2 = ((f32[128,8,128]{2,1,0:T(8,128)}), f32[128,8,128]{2,1,0:T(8,128)S(1)}, u32[]{:S(2)}, u32[]{:S(2)}) async-start(f32[128,8,128]{2,1,0:T(8,128)} %bitcast.51), calls=%async_computation.2 | async-start | bytes 1048576 | tf_op jit(solution)/shard_map/all_to_all | solution.py:105
  59.8 2.2 %all-to-all-done.2 = f32[128,8,128]{2,1,0:T(8,128)S(1)} async-done(((f32[128,8,128]{2,1,0:T(8,128)}), f32[128,8,128]{2,1,0:T(8,128)S(1)}, u32[]{:S(2)}, u32[]{:S(2)}) %all-to-all-start.2) | async-done | bytes 524320 | tf_op jit(solution)/shard_map/all_to_all | solution.py:105
  73.9 8.2 %all_to_all.102 = f32[2,1,65536]{2,1,0:T(1,128)S(1)} all-to-all(f32[2,1,65536]{2,1,0:T(1,128)S(1)} %reshape.112), channel_id=1, replica_groups=mesh['wide'=16,'narrow'=2] {'narrow'}, dimensions={0} | all-to-all | bytes 1048576 | tf_op jit(solution)/shard_map/all_to_all | solution.py:113
  82.5 2.3 %reduce = f32[2,65536]{1,0:T(2,128)S(1)} reduce(f32[2,1,65536]{2,1,0:T(1,128)S(1)} %all_to_all.102, f32[]{:T(128)} %broadcast.303), dimensions={1}, to_apply=%all_to_all.88.reduce_sub_computation | reduce | bytes 1048580 | tf_op jit(solution)/shard_map/all_to_all | solution.py:113
  86.0 22.1 %all_to_all.103 = f32[128,8,128]{2,1,0:T(8,128)S(1)} all-to-all(f32[128,8,128]{2,1,0:T(8,128)S(1)} %bitcast.188), channel_id=1, replica_groups=mesh['wide'=16,'narrow'=2] {'wide'}, dimensions={0} | all-to-all | bytes 1048576 | tf_op jit(solution)/shard_map/all_to_all | solution.py:112
  108.7 2.4 %collective-permute-start = (f32[2,128,1,128]{3,2,1,0:T(1,128)S(1)}, f32[2,128,1,128]{3,2,1,0:T(1,128)S(1)}, u32[]{:S(2)}, u32[]{:S(2)}) collective-permute-start(f32[2,128,1,128]{3,2,1,0:T(1,128)S(1)} %get-tuple-element.31), channel_id=1, source_target_pairs={{0,2},{2,4},{4,6},{6,8},{8,10},{10,12},{12,14},{14,16},{16,18},{18... | collective-permute-start | bytes 393224 | tf_op jit(solution)/shard_map/ppermute | solution.py:17
  111.1 1.9 %collective-permute-start.1 = (f32[2,128,1,128]{3,2,1,0:T(1,128)S(1)}, f32[2,128,1,128]{3,2,1,0:T(1,128)S(1)}, u32[]{:S(2)}, u32[]{:S(2)}) collective-permute-start(f32[2,128,1,128]{3,2,1,0:T(1,128)S(1)} %get-tuple-element.32), channel_id=1, source_target_pairs={{2,0},{4,2},{6,4},{8,6},{10,8},{12,10},{14,12},{16,14},{18,16},{20... | collective-permute-start | bytes 393224 | tf_op jit(solution)/shard_map/ppermute | solution.py:19
  113.0 4.3 %collective-permute-done.1 = f32[2,128,1,128]{3,2,1,0:T(1,128)S(1)} collective-permute-done((f32[2,128,1,128]{3,2,1,0:T(1,128)S(1)}, f32[2,128,1,128]{3,2,1,0:T(1,128)S(1)}, u32[]{:S(2)}, u32[]{:S(2)}) %collective-permute-start.1) | collective-permute-done | bytes 131104 | tf_op jit(solution)/shard_map/ppermute | solution.py:19
  117.7 2.0 %fusion.90 = (f32[2,128,10,1]{3,2,1,0:T(8,128)}, f32[2,128,10,1]{3,2,1,0:T(8,128)S(1)}) fusion(f32[2,128,10,128]{3,2,1,0:T(8,128)S(1)} %pad_maximum_fusion), kind=kLoop, calls=%fused_computation.290 | loop fusion | bytes 40960 | tf_op jit(solution)/shard_map/slice | solution.py:14
  119.8 2.2 %copy.453 = f32[2,128,10,1]{1,0,3,2:T(2,128)S(1)} copy(f32[2,128,10,1]{3,2,1,0:T(8,128)} %get-tuple-element.25) | data formatting | bytes 20480 | tf_op jit(solution)/shard_map/slice | solution.py:14
  122.0 2.1 %collective-permute-start.2 = (f32[2,128,10,1]{1,0,3,2:T(2,128)S(1)}, f32[2,128,10,1]{1,0,3,2:T(2,128)S(1)}, u32[]{:S(2)}, u32[]{:S(2)}) collective-permute-start(f32[2,128,10,1]{1,0,3,2:T(2,128)S(1)} %copy.453), channel_id=1, source_target_pairs={{0,1},{2,3},{4,5},{6,7},{8,9},{10,11},{12,13},{14,15},{16,17},{18,... | collective-permute-start | bytes 30728 | tf_op jit(solution)/shard_map/ppermute | solution.py:17
  127.0 2.2 %collective-permute-done.3 = f32[2,128,10,1]{1,0,3,2:T(2,128)S(1)} collective-permute-done((f32[2,128,10,1]{1,0,3,2:T(2,128)S(1)}, f32[2,128,10,1]{1,0,3,2:T(2,128)S(1)}, u32[]{:S(2)}, u32[]{:S(2)}) %collective-permute-start.3) | collective-permute-done | bytes 10272 | tf_op jit(solution)/shard_map/ppermute | solution.py:19
  129.2 2.1 %copy.456 = f32[2,128,10,1]{3,2,1,0:T(8,128)} copy(f32[2,128,10,1]{1,0,3,2:T(2,128)S(1)} %collective-permute-done.3) | data formatting | bytes 20480 | tf_op jit(solution)/shard_map/ppermute | solution.py:19
  131.3 5.2 %select_maximum_fusion = f32[2,130,10,130]{3,2,1,0:T(8,128)S(1)} fusion(f32[2,128,10,1]{3,2,1,0:T(8,128)} %copy.456, f32[2,128,10,1]{3,2,1,0:T(8,128)S(1)} %copy.455, f32[2,128,1,128]{3,2,1,0:T(1,128)S(1)} %collective-permute-done.1, f32[2,128,1,128]{3,2,1,0:T(1,128)S(1)} %collective-permute-done, f32[1,128,8,128]{3,2,1,0:T(8,128)S(1)} %bitcast.162, ...), kind=kLoop, calls=%fused_computation.2 | loop fusion | flops 4732000 | bytes 2683200 | tf_op jit(solution)/shard_map/concatenate | solution.py:15
  136.5 1.8 %slice_bitcast_fusion.1 = (f32[130,10,130]{2,1,0:T(8,128)S(1)}, f32[130,10,130]{2,1,0:T(8,128)}) fusion(f32[2,130,10,130]{3,2,1,0:T(8,128)S(1)} %select_maximum_fusion), kind=kLoop, calls=%fused_computation.9 | loop fusion | bytes 2704000 | tf_op jit(solution)/shard_map/squeeze | solution.py:66
  138.4 7.9 %fusion.15 = f32[128,8,128]{2,1,0:T(8,128)} fusion(f32[128,8,128]{2,1,0:T(8,128)S(1)} %copy-done.6, f32[130,10,130]{2,1,0:T(8,128)} %get-tuple-element.24, f32[130,10,130]{2,1,0:T(8,128)S(1)} %get-tuple-element.23), kind=kLoop, calls=%fused_computation.32 | loop fusion | flops 3932160 | bytes 8388608 | tf_op jit(solution)/shard_map/add | solution.py:123
  (331 shorter events, 26.5 us)
Async XLA Ops:
  0.6 9.2 %copy-start.7 = (f32[128,8,128]{2,1,0:T(8,128)S(1)}, f32[128,8,128]{2,1,0:T(8,128)}, u32[]{:S(2)}) copy-start(f32[128,8,128]{2,1,0:T(8,128)} %param.7) | copy-start | bytes 1572868
  0.6 21.6 %all-to-all-start.1 = ((f32[8,128,128]{2,0,1:T(8,128)}), f32[8,128,128]{2,0,1:T(8,128)S(1)}, u32[]{:S(2)}, u32[]{:S(2)}) async-start(f32[8,128,128]{2,0,1:T(8,128)} %bitcast.159), calls=%async_computation.1 | async-start | bytes 1048576 | tf_op jit(solution)/shard_map/all_to_all | solution.py:95
  22.2 18.6 %all-to-all-start = ((f32[8,128,128]{2,0,1:T(8,128)}), f32[8,128,128]{2,0,1:T(8,128)S(1)}, u32[]{:S(2)}, u32[]{:S(2)}) async-start(f32[8,128,128]{2,0,1:T(8,128)} %bitcast.21), calls=%async_computation | async-start | bytes 1048576 | tf_op jit(solution)/shard_map/all_to_all | solution.py:92
  40.8 11.1 %all-to-all-start.3 = ((f32[128,8,128]{2,1,0:T(8,128)}), f32[128,8,128]{2,1,0:T(8,128)S(1)}, u32[]{:S(2)}, u32[]{:S(2)}) async-start(f32[128,8,128]{2,1,0:T(8,128)} %bitcast.29), calls=%async_computation.3 | async-start | bytes 1048576 | tf_op jit(solution)/shard_map/all_to_all | solution.py:106
  51.9 10.2 %all-to-all-start.2 = ((f32[128,8,128]{2,1,0:T(8,128)}), f32[128,8,128]{2,1,0:T(8,128)S(1)}, u32[]{:S(2)}, u32[]{:S(2)}) async-start(f32[128,8,128]{2,1,0:T(8,128)} %bitcast.51), calls=%async_computation.2 | async-start | bytes 1048576 | tf_op jit(solution)/shard_map/all_to_all | solution.py:105
  62.0 3.8 %copy-start.2 = (f32[128,512]{1,0:T(8,128)S(1)}, f32[128,512]{1,0:T(8,128)}, u32[]{:S(2)}) copy-start(f32[128,512]{1,0:T(8,128)} %slice.1130) | copy-start | bytes 786436
  62.1 3.8 %copy-start.3 = (f32[128,512]{1,0:T(8,128)S(1)}, f32[128,512]{1,0:T(8,128)}, u32[]{:S(2)}) copy-start(f32[128,512]{1,0:T(8,128)} %slice.1119) | copy-start | bytes 786436
  64.0 1.9 %copy-start.4 = (f32[128,512]{1,0:T(8,128)S(1)}, f32[128,512]{1,0:T(8,128)}, u32[]{:S(2)}) copy-start(f32[128,512]{1,0:T(8,128)} %slice.1118) | copy-start | bytes 786436
  85.5 22.7 %copy-start.5 = (f32[128,8,128]{2,1,0:T(8,128)S(1)}, f32[128,8,128]{2,1,0:T(8,128)}, u32[]{:S(2)}) copy-start(f32[128,8,128]{2,1,0:T(8,128)} %param.4) | copy-start | bytes 1572868
  85.9 22.6 %copy-start = (f32[128,8,128]{2,1,0:T(8,128)S(1)}, f32[128,8,128]{2,1,0:T(8,128)}, u32[]{:S(2)}) copy-start(f32[128,8,128]{2,1,0:T(8,128)} %param.5) | copy-start | bytes 1572868
  108.5 22.8 %copy-start.1 = (f32[128,8,128]{2,1,0:T(8,128)}, f32[128,8,128]{2,1,0:T(8,128)S(1)}, u32[]{:S(2)}) copy-start(f32[128,8,128]{2,1,0:T(8,128)S(1)} %bitcast_add_fusion) | copy-start | bytes 1572868
  108.7 4.3 %collective-permute-start = (f32[2,128,1,128]{3,2,1,0:T(1,128)S(1)}, f32[2,128,1,128]{3,2,1,0:T(1,128)S(1)}, u32[]{:S(2)}, u32[]{:S(2)}) collective-permute-start(f32[2,128,1,128]{3,2,1,0:T(1,128)S(1)} %get-tuple-element.31), channel_id=1, source_target_pairs={{0,2},{2,4},{4,6},{6,8},{8,10},{10,12},{12,14},{14,16},{16,18},{18... | collective-permute-start | bytes 393224 | tf_op jit(solution)/shard_map/ppermute | solution.py:17
  111.1 6.3 %collective-permute-start.1 = (f32[2,128,1,128]{3,2,1,0:T(1,128)S(1)}, f32[2,128,1,128]{3,2,1,0:T(1,128)S(1)}, u32[]{:S(2)}, u32[]{:S(2)}) collective-permute-start(f32[2,128,1,128]{3,2,1,0:T(1,128)S(1)} %get-tuple-element.32), channel_id=1, source_target_pairs={{2,0},{4,2},{6,4},{8,6},{10,8},{12,10},{14,12},{16,14},{18,16},{20... | collective-permute-start | bytes 393224 | tf_op jit(solution)/shard_map/ppermute | solution.py:19
  122.0 4.1 %collective-permute-start.2 = (f32[2,128,10,1]{1,0,3,2:T(2,128)S(1)}, f32[2,128,10,1]{1,0,3,2:T(2,128)S(1)}, u32[]{:S(2)}, u32[]{:S(2)}) collective-permute-start(f32[2,128,10,1]{1,0,3,2:T(2,128)S(1)} %copy.453), channel_id=1, source_target_pairs={{0,1},{2,3},{4,5},{6,7},{8,9},{10,11},{12,13},{14,15},{16,17},{18,... | collective-permute-start | bytes 30728 | tf_op jit(solution)/shard_map/ppermute | solution.py:17
  124.8 4.4 %collective-permute-start.3 = (f32[2,128,10,1]{1,0,3,2:T(2,128)S(1)}, f32[2,128,10,1]{1,0,3,2:T(2,128)S(1)}, u32[]{:S(2)}, u32[]{:S(2)}) collective-permute-start(f32[2,128,10,1]{1,0,3,2:T(2,128)S(1)} %copy.454), channel_id=1, source_target_pairs={{1,0},{3,2},{5,4},{7,6},{9,8},{11,10},{13,12},{15,14},{17,16},{19,... | collective-permute-start | bytes 30728 | tf_op jit(solution)/shard_map/ppermute | solution.py:19
  136.5 1.8 %copy-start.6 = (f32[128,8,128]{2,1,0:T(8,128)S(1)}, f32[128,8,128]{2,1,0:T(8,128)}, u32[]{:S(2)}) copy-start(f32[128,8,128]{2,1,0:T(8,128)} %param.6) | copy-start | bytes 1572868
where the time goes:
time: 148 us; the launch traced here: 146 us
  waiting for transfers between devices  34.4 us (23%)
  blocking collectives  30.3 us (20%)
  local copies, waits for them, and re-layouts  27.9 us (19%)
  starting transfers between devices  26.7 us (18%)
  other arithmetic  24.2 us (16%)
  between operations  2.76 us (2%)
    all_to_all x1, blocking collectives, per_device(): lax.all_to_all(lax.all_to_all(third_block, 'narrow', split_axis=2, concat...  22.1 us
    all_to_all x1, waiting for transfers between devices, per_device(): lax.all_to_all(jnp.swapaxes(first, 0, 1), 'wide', split_axis=1, concat_ax...  11.3 us
    all_to_all x1, waiting for transfers between devices, per_device(): lax.all_to_all(jnp.swapaxes(diffusivity_coefficient, 0, 1), 'wide', split...  9.46 us
    all_to_all x1, blocking collectives, per_device(): lax.all_to_all(third_block, 'narrow', split_axis=2, concat_axis=0, tiled=...  8.16 us
    add x1, other arithmetic, per_device(): heating_supply + operator(padded_pair(ghost_padded))  7.86 us
    all_to_all x1, starting transfers between devices, per_device(): lax.all_to_all(jnp.swapaxes(diffusivity_coefficient, 0, 1), 'wide', split...  7.49 us
    ppermute x2, waiting for transfers between devices, extended(): lax.ppermute(head, axis, [((i + 1) % count, i) for i in range(ends)])  6.51 us
    concatenate x2, other arithmetic, extended(): jnp.concatenate([lax.ppermute(tail, axis, [(i, (i + 1) % count) for i in...  5.6 us
  transfers between devices with their start and end apart: 8, of which 6 were waited for; matrix products, arithmetic and copies ran while one was open for 10% of the time, Pallas kernels for 0%

commit v1 on v0

v1 whole, which is shorter than its diff:
```python
import jax
import jax.numpy as jnp
from jax import lax
from jax.experimental import pallas as pl
from jax.experimental.pallas import tpu as pltpu
from jax.sharding import PartitionSpec as P

HALF = 256
HH = 0.5 * HALF
CELLS = 8
F32 = jnp.float32
MESH = pl.DeviceIdType.MESH


def factor(cs, lo, hi):
    n = len(cs)
    q, inv = [], []
    e = 1.0 + lo * cs[0]
    for i in range(n - 1):
        w = HH * (cs[i] + cs[i + 1])
        iv = 1.0 / (e + w)
        inv.append(iv)
        q.append(w * iv)
        e = 1.0 + q[i] * e
        if i == n - 2:
            e = e + hi * cs[n - 1]
    inv.append(1.0 / e)
    s = [None] * n
    s[1] = q[0]
    for i in range(2, n):
        s[i] = s[i - 1] * q[i - 1]
    first, last = [None] * n, [None] * n
    last[n - 1] = inv[n - 1]
    first[n - 1] = s[n - 1] * inv[n - 1]
    for i in range(n - 2, -1, -1):
        last[i] = q[i] * last[i + 1]
        first[i] = (inv[i] if i == 0 else s[i] * inv[i]) + q[i] * first[i + 1]
    return q, inv, first, last


def substitute(rs, q, inv):
    n = len(rs)
    s = [rs[0]]
    for i in range(1, n):
        s.append(rs[i] + q[i - 1] * s[i - 1])
    h = [None] * n
    h[n - 1] = s[n - 1] * inv[n - 1]
    for i in range(n - 2, -1, -1):
        h[i] = s[i] * inv[i] + q[i] * h[i + 1]
    return h


def chain_factor(diag, off):
    m, k = [], []
    for p in range(len(diag)):
        d = diag[p] if p == 0 else diag[p] - k[p - 1] * off[p - 1]
        m.append(1.0 / d)
        if p < len(off):
            k.append(m[p] * off[p])
    return m, k


def chain_solve(rhs, m, k):
    n = len(rhs)
    s = [rhs[0]]
    for p in range(1, n):
        s.append(rhs[p] + k[p - 1] * s[p - 1])
    f = [None] * n
    f[n - 1] = m[n - 1] * s[n - 1]
    for p in range(n - 2, -1, -1):
        f[p] = m[p] * s[p] + k[p] * f[p + 1]
    return f


def make_kernel(W, N, X, Y, Z):
    R = X // W
    XB, ZB = X // CELLS, Z // CELLS

    def row(ref, j):
        j = j * Y
        if not isinstance(j, int):
            j = pl.multiple_of(j, Y)
        return ref[pl.ds(j, Y), :]

    def put(ref, j, v):
        j = j * Y
        if not isinstance(j, int):
            j = pl.multiple_of(j, Y)
        ref[pl.ds(j, Y), :] = v

    def loop(count, body, unroll):
        def step(i, c):
            for u in range(unroll):
                body(i * unroll + u)
            return c
        lax.fori_loop(0, count // unroll, step, 0)

    def line_op(c_ref, v_ref, g, count, c_lo, v_lo, c_hi, v_hi):
        base = g * CELLS
        before = jnp.maximum(base - 1, 0)
        after = jnp.minimum(base + CELLS, count * CELLS - 1)
        cs = [row(c_ref, base + i) for i in range(CELLS)]
        vs = [row(v_ref, base + i) for i in range(CELLS)]
        cs = [jnp.where(g == 0, c_lo, row(c_ref, before))] + cs
        vs = [jnp.where(g == 0, v_lo, row(v_ref, before))] + vs
        cs.append(jnp.where(g == count - 1, c_hi, row(c_ref, after)))
        vs.append(jnp.where(g == count - 1, v_hi, row(v_ref, after)))
        fl = [0.5 * (cs[i] + cs[i + 1]) * (vs[i + 1] - vs[i]) for i in range(CELLS + 1)]
        return [fl[i + 1] - fl[i] for i in range(CELLS)]

    def kernel(init, cond, heat, known, adv, upc,
               hx, v1x, v8x, fx, first,
               cy, qy, iy, v1y, v8y, hy, sec,
               msend, mrecv, rsend, rrecv, sm, sk, fs, frecv,
               cz, iz, qz, nz_, v1z, v8z, hz, rz, fz, az, bz, mz, kz,
               zmat, zrhs, zf, lz, advy, chs, chr_, ahr,
               ms_s, ms_r, rs_s, rs_r, fs_s, fs_r, zm_s, zm_r, zr_s, zr_r, ch_s, ch_r, ah_s, ah_r):
        me = lax.axis_index("wide")
        mine = lax.axis_index("narrow")
        up = lax.rem(me + 1, W)
        down = lax.rem(me + W - 1, W)

        barrier = pltpu.get_barrier_semaphore()

        def greet(o, c):
            pl.semaphore_signal(barrier, inc=1, device_id={"wide": lax.rem(me + o, W)}, device_id_type=MESH)
            return c
        lax.fori_loop(1, W, greet, 0)
        for o in range(1, N):
            pl.semaphore_signal(barrier, inc=1, device_id={"narrow": lax.rem(mine + o, N)}, device_id_type=MESH)

        def remote(src, dst, ss, rs, **dev):
            return pltpu.make_async_remote_copy(
                src_ref=src, dst_ref=dst, send_sem=ss, recv_sem=rs, device_id=dev, device_id_type=MESH)

        lo_y = jnp.where(me == 0, HH, 0.0).astype(F32)
        hi_y = jnp.where(me == W - 1, HH, 0.0).astype(F32)

        def rows(s):
            return pl.ds(s * R, R)

        def strided(s, y):
            return pl.ds(s * (R * Y) + y, R, stride=Y)

        def y_matrix(s):
            cs = [cond[strided(s, y), :] for y in range(Y)]
            q, inv, a, b = factor(cs, lo_y, hi_y)
            for y in range(Y):
                cy[y, rows(s), :] = cs[y]
                if y < Y - 1:
                    qy[y, rows(s), :] = q[y]
                iy[y, rows(s), :] = inv[y]
                v1y[y, rows(s), :] = a[y]
                v8y[y, rows(s), :] = b[y]
        loop(W, y_matrix, 4)

        pl.semaphore_wait(barrier, W - 1 + N - 1)

        to_up = lambda src, dst, ss, rs: remote(src, dst.at[0], ss.at[0], rs.at[0], wide=up)
        to_down = lambda src, dst, ss, rs: remote(src, dst.at[1], ss.at[1], rs.at[1], wide=down)
        c_up = to_up(cy.at[Y - 1], chr_, ch_s, ch_r)
        c_down = to_down(cy.at[0], chr_, ch_s, ch_r)

        def start_pair(a, b):
            @pl.when(me < W - 1)
            def _():
                a.start()

            @pl.when(me > 0)
            def _():
                b.start()

        def recv_pair(a, b):
            @pl.when(me > 0)
            def _():
                a.wait_recv()

            @pl.when(me < W - 1)
            def _():
                b.wait_recv()

        def sent_pair(a, b):
            @pl.when(me < W - 1)
            def _():
                a.wait_send()

            @pl.when(me > 0)
            def _():
                b.wait_send()

        start_pair(c_up, c_down)

        def zero_ends(ref):
            @pl.when(me == 0)
            def _():
                ref[0] = jnp.zeros((X, Z), F32)

            @pl.when(me == W - 1)
            def _():
                ref[1] = jnp.zeros((X, Z), F32)
        zero_ends(chr_)
        zero_ends(ahr)

        def x_blocks(b):
            lo = jnp.where(b == 0, HH, 0.0).astype(F32)
            hi = jnp.where(b == XB - 1, HH, 0.0).astype(F32)
            cs = [row(cond, b * CELLS + i) for i in range(CELLS)]
            rs = [(2.0 * HALF) * row(known, b * CELLS + i) for i in range(CELLS)]
            q, inv, u, v = factor(cs, lo, hi)
            h = substitute(rs, q, inv)
            for i in range(CELLS):
                put(hx, b * CELLS + i, h[i])
                put(v1x, b * CELLS + i, u[i])
                put(v8x, b * CELLS + i, v[i])
        loop(XB, x_blocks, 4)

        recv_pair(c_up, c_down)

        def fill(s):
            w = HH * (chr_[0, rows(s), :] + cy[0, rows(s), :])
            msend[s, 0] = v1y[0, rows(s), :] + 1.0 / w
            msend[s, 1] = v8y[Y - 1, rows(s), :]
            msend[s, 2] = v8y[0, rows(s), :]
        loop(W, fill, 4)

        def exchange(send, recv, ss, rs, pick):
            def step(o, c):
                to = lax.rem(me + o, W)
                remote(pick(send, to), recv.at[me], ss.at[o], rs.at[o], wide=to).start()
                return c
            lax.fori_loop(1, W, step, 0)

        def arrived(send, recv, ss, rs, pick):
            def step(o, c):
                frm = lax.rem(me + W - o, W)
                remote(pick(send, frm), recv.at[frm], ss.at[o], rs.at[o], wide=frm).wait_recv()
                return c
            lax.fori_loop(1, W, step, 0)

        def left(send, recv, ss, rs, pick):
            def step(o, c):
                to = lax.rem(me + o, W)
                remote(pick(send, to), recv.at[me], ss.at[o], rs.at[o], wide=to).wait_send()
                return c
            lax.fori_loop(1, W, step, 0)

        one = lambda ref, s: ref.at[s]
        two = lambda ref, s: ref.at[pl.ds(s, 2)]
        exchange(msend, mrecv, ms_s, ms_r, one)
        mrecv[me] = msend[me]

        def inner(c_ref, a_ref, b_ref, blocks):
            diag, off = [], []
            for p in range(1, blocks):
                j = p * CELLS
                w = HH * (row(c_ref, j - 1) + row(c_ref, j))
                diag.append(1.0 / w + row(b_ref, j - 1) + row(a_ref, j))
                if p < blocks - 1:
                    off.append(row(b_ref, j))
            return chain_factor(diag, off)

        zero = jnp.zeros((Y, Z), F32)
        m, k = inner(cond, v1x, v8x, XB)
        f = chain_solve([row(hx, p * CELLS - 1) - row(hx, p * CELLS) for p in range(1, XB)], m, k)
        fx[0] = zero
        fx[XB] = zero
        for p in range(1, XB):
            fx[p] = f[p - 1]

        def x_final(b):
            fl, fr = fx[b], fx[b + 1]
            for i in range(CELLS):
                j = b * CELLS + i
                put(first, j, row(hx, j) + row(v1x, j) * fl - row(v8x, j) * fr)
        loop(XB, x_final, 4)

        def y_rhs(s):
            rs = [first[strided(s, y), :] for y in range(Y)]
            h = substitute(rs, [qy[y, rows(s), :] for y in range(Y - 1)], [iy[y, rows(s), :] for y in range(Y)])
            for y in range(Y):
                hy[y, rows(s), :] = h[y]
            rsend[s, 0] = h[0]
            rsend[s, 1] = h[Y - 1]
        loop(W, y_rhs, 4)
        exchange(rsend, rrecv, rs_s, rs_r, one)
        rrecv[me] = rsend[me]

        for y in range(Y):
            cz[pl.ds(y, Z, stride=Y), :] = cy[y].T
            iz[pl.ds(y, Z, stride=Y), :] = init[pl.ds(y, X, stride=Y), :].T
        lo_z = jnp.where(mine == 0, HH, 0.0).astype(F32)
        hi_z = jnp.where(mine == N - 1, HH, 0.0).astype(F32)

        def z_blocks(b):
            lo = jnp.where(b == 0, lo_z, 0.0)
            hi = jnp.where(b == ZB - 1, hi_z, 0.0)
            cs = [row(cz, b * CELLS + i) for i in range(CELLS)]
            q, inv, u, v = factor(cs, lo, hi)
            for i in range(CELLS):
                j = b * CELLS + i
                if i < CELLS - 1:
                    put(qz, j, q[i])
                put(nz_, j, inv[i])
                put(v1z, j, u[i])
                put(v8z, j, v[i])
        loop(ZB, z_blocks, 4)
        m, k = inner(cz, v1z, v8z, ZB)
        n = ZB - 1
        for p in range(n):
            mz[p] = m[p]
            if p < n - 1:
                kz[p] = k[p]
        g18_lo, g18_hi = row(v8z, 0), row(v8z, (ZB - 1) * CELLS)
        a = chain_solve([g18_lo] + [zero] * (n - 1), m, k)
        b = [None] * n
        b[n - 1] = m[n - 1] * g18_hi
        for p in range(n - 2, -1, -1):
            b[p] = k[p] * b[p + 1]
        for p in range(n):
            az[p + 1] = a[p]
            bz[p + 1] = b[p]
        one_plane = jnp.ones((Y, Z), F32)
        az[0], bz[0] = one_plane, zero
        az[ZB], bz[ZB] = zero, one_plane
        zmat[mine, 0] = row(v1z, 0) - g18_lo * a[0]
        zmat[mine, 1] = row(v8z, Z - 1) - g18_hi * b[n - 1]
        zmat[mine, 2] = g18_hi * a[n - 1]
        zmat[mine, 3] = row(cz, 0)
        zmat[mine, 4] = row(cz, Z - 1)
        zmat[mine, 5] = row(iz, 0)
        zmat[mine, 6] = row(iz, Z - 1)

        def z_copy(buf, ss, rs, o, who, slot):
            return remote(buf.at[slot], buf.at[slot], ss.at[o], rs.at[o], narrow=who)

        def z_send(buf, ss, rs):
            for o in range(1, N):
                z_copy(buf, ss, rs, o, lax.rem(mine + o, N), mine).start()

        def z_recv(buf, ss, rs):
            for o in range(1, N):
                frm = lax.rem(mine + N - o, N)
                z_copy(buf, ss, rs, o, frm, frm).wait_recv()

        def z_left(buf, ss, rs):
            for o in range(1, N):
                z_copy(buf, ss, rs, o, lax.rem(mine + o, N), mine).wait_send()
        z_send(zmat, zm_s, zm_r)

        arrived(msend, mrecv, ms_s, ms_r, one)
        m, k = chain_factor(
            [mrecv[p, 0] + mrecv[p - 1, 1] for p in range(1, W)], [mrecv[p, 2] for p in range(1, W - 1)])
        for p in range(W - 1):
            sm[p] = m[p]
            if p < W - 2:
                sk[p] = k[p]

        z_recv(zmat, zm_s, zm_r)
        below, above = jnp.maximum(mine - 1, 0), jnp.minimum(mine + 1, N - 1)
        has_lo = jnp.where(mine > 0, 1.0, 0.0).astype(F32)
        has_hi = jnp.where(mine < N - 1, 1.0, 0.0).astype(F32)
        z_c_lo, z_v_lo = has_lo * zmat[below, 4], has_lo * zmat[below, 6]
        z_c_hi, z_v_hi = has_hi * zmat[above, 3], has_hi * zmat[above, 5]

        def z_old(g):
            out = line_op(cz, iz, g, ZB, z_c_lo, z_v_lo, z_c_hi, z_v_hi)
            for i in range(CELLS):
                put(rz, g * CELLS + i, out[i])
        loop(ZB, z_old, 2)
        for y in range(Y):
            lz[y] = rz[pl.ds(y, Z, stride=Y), :].T

        arrived(rsend, rrecv, rs_s, rs_r, one)
        f = chain_solve(
            [rrecv[p - 1, 1] - rrecv[p, 0] for p in range(1, W)],
            [sm[p] for p in range(W - 1)], [sk[p] for p in range(W - 2)])
        edge = jnp.zeros((R, Z), F32)
        fs[0] = edge
        fs[W] = edge
        for p in range(1, W):
            fs[p] = f[p - 1]
        exchange(fs, frecv, fs_s, fs_r, two)
        frecv[me] = fs[pl.ds(me, 2)]
        arrived(fs, frecv, fs_s, fs_r, two)

        def y_final(s):
            fl, fr = frecv[s, 0], frecv[s, 1]
            for y in range(Y):
                sec[y, rows(s), :] = hy[y, rows(s), :] + v1y[y, rows(s), :] * fl - v8y[y, rows(s), :] * fr
        loop(W, y_final, 4)
        for y in range(Y):
            rz[pl.ds(y, Z, stride=Y), :] = sec[y].T

        def z_rhs(b):
            j = b * CELLS
            h = substitute([row(rz, j + i) for i in range(CELLS)], [row(qz, j + i) for i in range(CELLS - 1)],
                           [row(nz_, j + i) for i in range(CELLS)])
            for i in range(CELLS):
                put(hz, j + i, h[i])
        loop(ZB, z_rhs, 4)
        f = chain_solve([row(hz, p * CELLS - 1) - row(hz, p * CELLS) for p in range(1, ZB)],
                        [mz[p] for p in range(n)], [kz[p] for p in range(n - 1)])
        for p in range(n):
            fz[p + 1] = f[p]
        fz[0] = zero
        fz[ZB] = zero
        zrhs[mine, 0] = row(hz, 0) - row(v8z, 0) * f[0]
        zrhs[mine, 1] = row(hz, Z - 1) + row(v8z, (ZB - 1) * CELLS) * f[n - 1]
        z_send(zrhs, zr_s, zr_r)
        m, k = chain_factor(
            [1.0 / (HH * (zmat[p - 1, 4] + zmat[p, 3])) + zmat[p - 1, 1] + zmat[p, 0] for p in range(1, N)],
            [zmat[p, 2] for p in range(1, N - 1)])
        z_recv(zrhs, zr_s, zr_r)
        f = chain_solve([zrhs[p - 1, 1] - zrhs[p, 0] for p in range(1, N)], m, k)
        zf[0] = zero
        zf[N] = zero
        for p in range(1, N):
            zf[p] = f[p - 1]
        z_fl, z_fr = zf[mine], zf[mine + 1]

        def z_final(b):
            fl = fz[b] + az[b] * z_fl + bz[b] * z_fr
            fr = fz[b + 1] + az[b + 1] * z_fl + bz[b + 1] * z_fr
            for i in range(CELLS):
                j = b * CELLS + i
                put(rz, j, row(hz, j) + row(v1z, j) * fl - row(v8z, j) * fr)
        loop(ZB, z_final, 4)

        a_up = to_up(advy.at[Y - 1], ahr, ah_s, ah_r)
        a_down = to_down(advy.at[0], ahr, ah_s, ah_r)

        def new_state(y):
            third = rz[pl.ds(y, Z, stride=Y), :].T
            state = init[pl.ds(y, X, stride=Y), :] + third
            advy[y] = state
            lz[y] = lz[y] + (third - sec[y]) * (1.0 / HALF)
            adv[pl.ds(y, X, stride=Y), :] = state
        new_state(0)
        new_state(Y - 1)
        start_pair(a_up, a_down)
        for y in range(1, Y - 1):
            new_state(y)

        def y_op(s):
            cs = [cy[y, rows(s), :] for y in range(Y)]
            vs = [advy[y, rows(s), :] for y in range(Y)]
            fl = [0.5 * (cs[i] + cs[i + 1]) * (vs[i + 1] - vs[i]) for i in range(Y - 1)]
            for y in range(Y):
                out = lz[y, rows(s), :]
                if y < Y - 1:
                    out = out + fl[y]
                if y > 0:
                    out = out - fl[y - 1]
                upc[strided(s, y), :] = out
        loop(W, y_op, 4)

        def x_op(g):
            out = line_op(cond, adv, g, XB, zero, zero, zero, zero)
            for i in range(CELLS):
                j = g * CELLS + i
                put(upc, j, row(upc, j) + (row(heat, j) + out[i]))
        loop(XB, x_op, 2)

        recv_pair(a_up, a_down)

        def y_ends(s):
            for slot, y in ((0, 0), (1, Y - 1)):
                fl = 0.5 * (chr_[slot, rows(s), :] + cy[y, rows(s), :]) * (ahr[slot, rows(s), :] - advy[y, rows(s), :])
                upc[strided(s, y), :] = upc[strided(s, y), :] + fl
        loop(W, y_ends, 4)

        sent_pair(c_up, c_down)
        sent_pair(a_up, a_down)
        left(msend, mrecv, ms_s, ms_r, one)
        left(rsend, rrecv, rs_s, rs_r, one)
        left(fs, frecv, fs_s, fs_r, two)
        z_left(zmat, zm_s, zm_r)
        z_left(zrhs, zr_s, zr_r)

    flat = pltpu.VMEM((X * Y, Z), F32)
    planes = pltpu.VMEM((Y, X, Z), F32)
    flux = lambda count: pltpu.VMEM((count, Y, Z), F32)
    part = lambda *lead: pltpu.VMEM((*lead, R, Z), F32)
    sems = lambda count: pltpu.SemaphoreType.DMA((count,))
    scratch = [flat, flat, flat, flux(XB + 1), flat,
               planes, planes, planes, planes, planes, planes, planes,
               part(W, 3), part(W, 3), part(W, 2), part(W, 2), part(W), part(W), part(W + 1), part(W, 2),
               flat, flat, flat, flat, flat, flat, flat, flat,
               flux(ZB + 1), flux(ZB + 1), flux(ZB + 1), flux(ZB), flux(ZB),
               pltpu.VMEM((N, 7, Y, Z), F32), pltpu.VMEM((N, 2, Y, Z), F32), flux(N + 1), planes, planes,
               pltpu.VMEM((8, Z), F32), pltpu.VMEM((2, X, Z), F32), pltpu.VMEM((2, X, Z), F32),
               sems(W), sems(W), sems(W), sems(W), sems(W), sems(W), sems(N), sems(N), sems(N), sems(N),
               sems(2), sems(2), sems(2), sems(2)]
    return kernel, scratch


def solution(mesh):
    W, N = mesh.shape["wide"], mesh.shape["narrow"]

    def per_device(*arrays):
        X, Y, Z = arrays[0].shape
        kernel, scratch = make_kernel(W, N, X, Y, Z)
        vmem = pl.BlockSpec(memory_space=pltpu.VMEM)
        out = jax.ShapeDtypeStruct((X * Y, Z), F32)
        results = pl.pallas_call(
            kernel,
            out_shape=(out, out),
            in_specs=[vmem] * 4,
            out_specs=(vmem, vmem),
            scratch_shapes=scratch,
            compiler_params=pltpu.CompilerParams(
                collective_id=0, has_side_effects=True, vmem_limit_bytes=48 * 1024 * 1024),
        )(*[a.reshape(X * Y, Z) for a in arrays])
        return tuple(r.reshape(X, Y, Z) for r in results)

    placed = P(None, "wide", "narrow")
    return jax.shard_map(
        per_device, mesh=mesh, in_specs=(placed,) * 4, out_specs=(placed, placed), check_vma=False)
```

time: 148 us -> 37.5 us (0.25); the launches traced: 146 us -> 37.2 us
  waiting for transfers between devices: 34.4 us -> 0 us
  Pallas kernels: 0 us -> 30.8 us
  blocking collectives: 30.3 us -> 0 us
  starting transfers between devices: 26.7 us -> 0 us
  other arithmetic: 24.2 us -> 0 us
  local copies, waits for them, and re-layouts: 27.9 us -> 5.75 us
  between operations: 2.76 us -> 0.65 us
    pallas_call x0 -> x1, Pallas kernels: none -> 30.8 us  [per_device(): pl.pallas_call(kernel, out_shape=(out, out), in_specs=[vmem] * 4, out_spe...]
    all_to_all x2 -> x0, blocking collectives: 30.3 us -> none  [the longest x1 22.1 us: per_device(): lax.all_to_all(lax.all_to_all(third_block, 'narrow', split_axis=2, concat...]
    all_to_all x4 -> x0, waiting for transfers between devices: 27.9 us -> none  [the longest x1 11.3 us: per_device(): lax.all_to_all(jnp.swapaxes(first, 0, 1), 'wide', split_axis=1, concat_ax...]
    all_to_all x4 -> x0, starting transfers between devices: 19 us -> none  [the longest x1 7.49 us: per_device(): lax.all_to_all(jnp.swapaxes(diffusivity_coefficient, 0, 1), 'wide', split...]
    slice x183 -> x0, local copies, waits for them, and re-layouts: 14.8 us -> none  [the longest x2 4.23 us: extended(): lax.slice_in_dim(cells, cells.shape[dim] - width, cells.shape[dim], axis=...]
    add x24 -> x0, other arithmetic: 14.4 us -> none  [the longest x1 7.86 us: per_device(): heating_supply + operator(padded_pair(ghost_padded))]
    ppermute x4 -> x0, starting transfers between devices: 7.7 us -> none  [the longest x2 4.49 us: extended(): lax.ppermute(tail, axis, [(i, (i + 1) % count) for i in range(ends)])]
    ppermute x4 -> x0, waiting for transfers between devices: 6.51 us -> none  [the longest x2 6.51 us: extended(): lax.ppermute(head, axis, [((i + 1) % count, i) for i in range(ends)])]
  transfers between devices with their start and end apart: 8 -> 0, of which waited for: 6 -> 0; matrix products, arithmetic and copies ran while one was open for 10% -> 0% of each run, Pallas kernels for 0% -> 0%
where the time goes in v1:
time: 37.5 us; the launch traced here: 37.2 us
  Pallas kernels  30.8 us (82%)
  local copies, waits for them, and re-layouts  5.75 us (15%)
  between operations  0.65 us (2%)
    pallas_call x1, Pallas kernels, per_device(): pl.pallas_call(kernel, out_shape=(out, out), in_specs=[vmem] * 4, out_spe...  30.8 us
    unnamed x10, local copies, waits for them, and re-layouts  5.75 us

profile of v1, /device:TPU:1, one launch (start us, length us, event | category | flops | bytes accessed | tf_op | source)
XLA Modules:
  0.0 37.2 jit_solution(15404885797294421409)
XLA Ops:
  0.6 0.0 copy-start
  0.6 1.0 %copy-done = f32[128,8,128]{2,1,0:T(8,128)S(1)} copy-done((f32[128,8,128]{2,1,0:T(8,128)S(1)}, f32[128,8,128]{2,1,0:T(8,128)}, u32[]{:S(2)}) %copy-start) | copy-done | bytes 524312
  1.7 0.0 copy-start.1
  1.7 1.0 %copy-done.1 = f32[128,8,128]{2,1,0:T(8,128)S(1)} copy-done((f32[128,8,128]{2,1,0:T(8,128)S(1)}, f32[128,8,128]{2,1,0:T(8,128)}, u32[]{:S(2)}) %copy-start.1) | copy-done | bytes 524312
  2.7 0.0 copy-start.2
  2.7 1.0 %copy-done.2 = f32[128,8,128]{2,1,0:T(8,128)S(1)} copy-done((f32[128,8,128]{2,1,0:T(8,128)S(1)}, f32[128,8,128]{2,1,0:T(8,128)}, u32[]{:S(2)}) %copy-start.2) | copy-done | bytes 524312
  3.8 0.0 copy-start.3
  3.8 1.0 %copy-done.3 = f32[128,8,128]{2,1,0:T(8,128)S(1)} copy-done((f32[128,8,128]{2,1,0:T(8,128)S(1)}, f32[128,8,128]{2,1,0:T(8,128)}, u32[]{:S(2)}) %copy-start.3) | copy-done | bytes 524312
  4.8 30.8 %shard_map.59 = (f32[1024,128]{1,0:T(8,128)S(1)}, f32[1024,128]{1,0:T(8,128)S(1)}) custom-call(f32[1024,128]{1,0:T(8,128)S(1)} %bitcast.8, f32[1024,128]{1,0:T(8,128)S(1)} %bitcast.9, f32[1024,128]{1,0:T(8,128)S(1)} %bitcast.10, f32[1024,128]{1,0:T(8,128)S(1)} %bitcast.11), custom_call_target="tpu_custom_call" | custom-call | tf_op jit(solution)/shard_map/pallas_call | solution.py:505
  35.6 0.8 %copy.8 = f32[128,8,128]{2,1,0:T(8,128)} copy(f32[128,8,128]{2,1,0:T(8,128)S(1)} %bitcast.7) | data formatting | bytes 1048576
  36.4 0.8 %copy.9 = f32[128,8,128]{2,1,0:T(8,128)} copy(f32[128,8,128]{2,1,0:T(8,128)S(1)} %bitcast.6) | data formatting | bytes 1048576
Async XLA Ops:
  0.6 1.0 %copy-start = (f32[128,8,128]{2,1,0:T(8,128)S(1)}, f32[128,8,128]{2,1,0:T(8,128)}, u32[]{:S(2)}) copy-start(f32[128,8,128]{2,1,0:T(8,128)} %param.4) | copy-start | bytes 1572868
  1.7 1.0 %copy-start.1 = (f32[128,8,128]{2,1,0:T(8,128)S(1)}, f32[128,8,128]{2,1,0:T(8,128)}, u32[]{:S(2)}) copy-start(f32[128,8,128]{2,1,0:T(8,128)} %param.5) | copy-start | bytes 1572868
  2.7 1.0 %copy-start.2 = (f32[128,8,128]{2,1,0:T(8,128)S(1)}, f32[128,8,128]{2,1,0:T(8,128)}, u32[]{:S(2)}) copy-start(f32[128,8,128]{2,1,0:T(8,128)} %param.6) | copy-start | bytes 1572868
  3.8 1.0 %copy-start.3 = (f32[128,8,128]{2,1,0:T(8,128)S(1)}, f32[128,8,128]{2,1,0:T(8,128)}, u32[]{:S(2)}) copy-start(f32[128,8,128]{2,1,0:T(8,128)} %param.7) | copy-start | bytes 1572868

commit v2 on v1

--- a/solution.py
+++ b/solution.py
@@ -108,13 +108,14 @@
         fl = [0.5 * (cs[i] + cs[i + 1]) * (vs[i + 1] - vs[i]) for i in range(CELLS + 1)]
         return [fl[i + 1] - fl[i] for i in range(CELLS)]
 
-    def kernel(init, cond, heat, known, adv, upc,
+    def kernel(init_h, cond_h, heat_h, known_h, adv, upc,
+               init, cond, heat, known,
                hx, v1x, v8x, fx, first,
                cy, qy, iy, v1y, v8y, hy, sec,
                msend, mrecv, rsend, rrecv, sm, sk, fs, frecv,
                cz, iz, qz, nz_, v1z, v8z, hz, rz, fz, az, bz, mz, kz,
                zmat, zrhs, zf, lz, advy, chs, chr_, ahr,
-               ms_s, ms_r, rs_s, rs_r, fs_s, fs_r, zm_s, zm_r, zr_s, zr_r, ch_s, ch_r, ah_s, ah_r):
+               ms_s, ms_r, rs_s, rs_r, fs_s, fs_r, zm_s, zm_r, zr_s, zr_r, ch_s, ch_r, ah_s, ah_r, in_s):
         me = lax.axis_index("wide")
         mine = lax.axis_index("narrow")
         up = lax.rem(me + 1, W)
@@ -129,6 +130,11 @@
         for o in range(1, N):
             pl.semaphore_signal(barrier, inc=1, device_id={"narrow": lax.rem(mine + o, N)}, device_id_type=MESH)
 
+        loads = [pltpu.make_async_copy(a, b, in_s.at[i]) for i, (a, b) in enumerate(
+            ((cond_h, cond), (known_h, known), (init_h, init), (heat_h, heat)))]
+        for load in loads:
+            load.start()
+
         def remote(src, dst, ss, rs, **dev):
             return pltpu.make_async_remote_copy(
                 src_ref=src, dst_ref=dst, send_sem=ss, recv_sem=rs, device_id=dev, device_id_type=MESH)
@@ -141,6 +147,8 @@
 
         def strided(s, y):
             return pl.ds(s * (R * Y) + y, R, stride=Y)
+
+        loads[0].wait()
 
         def y_matrix(s):
             cs = [cond[strided(s, y), :] for y in range(Y)]
@@ -154,8 +162,6 @@
                 v8y[y, rows(s), :] = b[y]
         loop(W, y_matrix, 4)
 
-        pl.semaphore_wait(barrier, W - 1 + N - 1)
-
         to_up = lambda src, dst, ss, rs: remote(src, dst.at[0], ss.at[0], rs.at[0], wide=up)
         to_down = lambda src, dst, ss, rs: remote(src, dst.at[1], ss.at[1], rs.at[1], wide=down)
         c_up = to_up(cy.at[Y - 1], chr_, ch_s, ch_r)
@@ -188,8 +194,6 @@
             def _():
                 b.wait_send()
 
-        start_pair(c_up, c_down)
-
         def zero_ends(ref):
             @pl.when(me == 0)
             def _():
@@ -201,6 +205,7 @@
         zero_ends(chr_)
         zero_ends(ahr)
 
+        loads[1].wait()
         def x_blocks(b):
             lo = jnp.where(b == 0, HH, 0.0).astype(F32)
             hi = jnp.where(b == XB - 1, HH, 0.0).astype(F32)
@@ -214,15 +219,6 @@
                 put(v8x, b * CELLS + i, v[i])
         loop(XB, x_blocks, 4)
 
-        recv_pair(c_up, c_down)
-
-        def fill(s):
-            w = HH * (chr_[0, rows(s), :] + cy[0, rows(s), :])
-            msend[s, 0] = v1y[0, rows(s), :] + 1.0 / w
-            msend[s, 1] = v8y[Y - 1, rows(s), :]
-            msend[s, 2] = v8y[0, rows(s), :]
-        loop(W, fill, 4)
-
         def exchange(send, recv, ss, rs, pick):
             def step(o, c):
                 to = lax.rem(me + o, W)
@@ -246,9 +242,6 @@
 
         one = lambda ref, s: ref.at[s]
         two = lambda ref, s: ref.at[pl.ds(s, 2)]
-        exchange(msend, mrecv, ms_s, ms_r, one)
-        mrecv[me] = msend[me]
-
         def inner(c_ref, a_ref, b_ref, blocks):
             diag, off = [], []
             for p in range(1, blocks):
@@ -282,9 +275,24 @@
             rsend[s, 0] = h[0]
             rsend[s, 1] = h[Y - 1]
         loop(W, y_rhs, 4)
+        pl.semaphore_wait(barrier, W - 1 + N - 1)
+        start_pair(c_up, c_down)
         exchange(rsend, rrecv, rs_s, rs_r, one)
         rrecv[me] = rsend[me]
 
+        recv_pair(c_up, c_down)
+
+        def fill(s):
+            w = HH * (chr_[0, rows(s), :] + cy[0, rows(s), :])
+            msend[s, 0] = v1y[0, rows(s), :] + 1.0 / w
+            msend[s, 1] = v8y[Y - 1, rows(s), :]
+            msend[s, 2] = v8y[0, rows(s), :]
+        loop(W, fill, 4)
+
+        exchange(msend, mrecv, ms_s, ms_r, one)
+        mrecv[me] = msend[me]
+
+        loads[2].wait()
         for y in range(Y):
             cz[pl.ds(y, Z, stride=Y), :] = cy[y].T
             iz[pl.ds(y, Z, stride=Y), :] = init[pl.ds(y, X, stride=Y), :].T
@@ -454,6 +462,8 @@
                 upc[strided(s, y), :] = out
         loop(W, y_op, 4)
 
+        loads[3].wait()
+
         def x_op(g):
             out = line_op(cond, adv, g, XB, zero, zero, zero, zero)
             for i in range(CELLS):
@@ -482,7 +492,7 @@
     flux = lambda count: pltpu.VMEM((count, Y, Z), F32)
     part = lambda *lead: pltpu.VMEM((*lead, R, Z), F32)
     sems = lambda count: pltpu.SemaphoreType.DMA((count,))
-    scratch = [flat, flat, flat, flux(XB + 1), flat,
+    scratch = [flat, flat, flat, flat, flat, flat, flat, flux(XB + 1), flat,
                planes, planes, planes, planes, planes, planes, planes,
                part(W, 3), part(W, 3), part(W, 2), part(W, 2), part(W), part(W), part(W + 1), part(W, 2),
                flat, flat, flat, flat, flat, flat, flat, flat,
@@ -490,7 +500,7 @@
                pltpu.VMEM((N, 7, Y, Z), F32), pltpu.VMEM((N, 2, Y, Z), F32), flux(N + 1), planes, planes,
                pltpu.VMEM((8, Z), F32), pltpu.VMEM((2, X, Z), F32), pltpu.VMEM((2, X, Z), F32),
                sems(W), sems(W), sems(W), sems(W), sems(W), sems(W), sems(N), sems(N), sems(N), sems(N),
-               sems(2), sems(2), sems(2), sems(2)]
+               sems(2), sems(2), sems(2), sems(2), sems(4)]
     return kernel, scratch
 
 
@@ -505,11 +515,11 @@
         results = pl.pallas_call(
             kernel,
             out_shape=(out, out),
-            in_specs=[vmem] * 4,
+            in_specs=[pl.BlockSpec(memory_space=pl.ANY)] * 4,
             out_specs=(vmem, vmem),
             scratch_shapes=scratch,
             compiler_params=pltpu.CompilerParams(
-                collective_id=0, has_side_effects=True, vmem_limit_bytes=48 * 1024 * 1024),
+                collective_id=0, has_side_effects=True, vmem_limit_bytes=56 * 1024 * 1024),
         )(*[a.reshape(X * Y, Z) for a in arrays])
         return tuple(r.reshape(X, Y, Z) for r in results)
 

time: 37.5 us -> 33.6 us (0.90)
  local copies, waits for them, and re-layouts: 5.75 us -> 2.72 us
  Pallas kernels: 30.8 us -> 30 us
    unnamed x10 -> x4, local copies, waits for them, and re-layouts: 5.75 us -> 2.72 us
    pallas_call x1, Pallas kernels: 30.8 us -> 30 us  [per_device(): pl.pallas_call(kernel, out_shape=(out, out), in_specs=[pl.BlockSpec(memor...]
where the time goes in v2:
time: 33.6 us; the launch traced here: 33.4 us
  Pallas kernels  30 us (89%)
  local copies, waits for them, and re-layouts  2.72 us (8%)
  between operations  0.65 us (2%)
    pallas_call x1, Pallas kernels, per_device(): pl.pallas_call(kernel, out_shape=(out, out), in_specs=[pl.BlockSpec(memor...  30 us
    unnamed x4, local copies, waits for them, and re-layouts  2.72 us

profile of v2, /device:TPU:1, one launch (start us, length us, event | category | flops | bytes accessed | tf_op | source)
XLA Modules:
  0.0 33.4 jit_solution(16913704056864085525)
XLA Ops:
  0.6 30.0 %shard_map.59 = (f32[1024,128]{1,0:T(8,128)}, f32[1024,128]{1,0:T(8,128)}) custom-call(f32[1024,128]{1,0:T(8,128)} %bitcast.8, f32[1024,128]{1,0:T(8,128)} %bitcast.9, f32[1024,128]{1,0:T(8,128)} %bitcast.10, f32[1024,128]{1,0:T(8,128)} %bitcast.11), custom_call_target="tpu_custom_call" | custom-call | tf_op jit(solution)/shard_map/pallas_call | solution.py:515
  30.7 0.0 copy-start
  30.7 1.9 %copy.8 = f32[128,8,128]{2,1,0:T(8,128)} copy(f32[128,8,128]{2,1,0:T(8,128)} %bitcast.7) | data formatting | bytes 1048576
  32.6 0.0 copy-done
  32.6 0.8 %copy.9 = f32[128,8,128]{2,1,0:T(8,128)} copy(f32[128,8,128]{2,1,0:T(8,128)S(1)} %bitcast.6) | data formatting | bytes 1048576
Async XLA Ops:
  30.7 1.9 %copy-start = (f32[1024,128]{1,0:T(8,128)S(1)}, f32[1024,128]{1,0:T(8,128)}, u32[]{:S(2)}) copy-start(f32[1024,128]{1,0:T(8,128)} %get-tuple-element.5) | copy-start | bytes 1572868

commit v3 on v2

--- a/solution.py
+++ b/solution.py
@@ -74,6 +74,8 @@
 
 def make_kernel(W, N, X, Y, Z):
     R = X // W
+    C = W // 2
+    H = X // 2
     XB, ZB = X // CELLS, Z // CELLS
 
     def row(ref, j):
@@ -112,12 +114,15 @@
                init, cond, heat, known,
                hx, v1x, v8x, fx, first,
                cy, qy, iy, v1y, v8y, hy, sec,
-               msend, mrecv, rsend, rrecv, sm, sk, fs, frecv,
+               xs, xr, bf, ba, bb, msend, mrecv, sm, sk, fs, frecv, ps, pr,
                cz, iz, qz, nz_, v1z, v8z, hz, rz, fz, az, bz, mz, kz,
-               zmat, zrhs, zf, lz, advy, chs, chr_, ahr,
-               ms_s, ms_r, rs_s, rs_r, fs_s, fs_r, zm_s, zm_r, zr_s, zr_r, ch_s, ch_r, ah_s, ah_r, in_s):
+               zmat, zrhs, zf, lz, advy, ccr, chr_, ahr,
+               ms_s, ms_r, fs_s, fs_r, xs_s, xs_r, ps_s, ps_r, cc_s, cc_r, zm_s, zm_r, zr_s, zr_r, ch_s, ch_r, ah_s, ah_r, in_s):
         me = lax.axis_index("wide")
         mine = lax.axis_index("narrow")
+        core = lax.rem(me, 2)
+        chip = me // 2
+        mate = chip * 2 + 1 - core
         up = lax.rem(me + 1, W)
         down = lax.rem(me + W - 1, W)
 
@@ -160,6 +165,8 @@
                 iy[y, rows(s), :] = inv[y]
                 v1y[y, rows(s), :] = a[y]
                 v8y[y, rows(s), :] = b[y]
+            for i, v in enumerate((a[0], b[0], b[Y - 1], cs[0], cs[Y - 1])):
+                xs[2 + i, rows(s), :] = v
         loop(W, y_matrix, 4)
 
         to_up = lambda src, dst, ss, rs: remote(src, dst.at[0], ss.at[0], rs.at[0], wide=up)
@@ -221,24 +228,24 @@
 
         def exchange(send, recv, ss, rs, pick):
             def step(o, c):
-                to = lax.rem(me + o, W)
-                remote(pick(send, to), recv.at[me], ss.at[o], rs.at[o], wide=to).start()
+                to = lax.rem(chip + o, C)
+                remote(pick(send, to), recv.at[chip], ss.at[o], rs.at[o], wide=2 * to + core).start()
                 return c
-            lax.fori_loop(1, W, step, 0)
+            lax.fori_loop(1, C, step, 0)
 
         def arrived(send, recv, ss, rs, pick):
             def step(o, c):
-                frm = lax.rem(me + W - o, W)
-                remote(pick(send, frm), recv.at[frm], ss.at[o], rs.at[o], wide=frm).wait_recv()
+                frm = lax.rem(chip + C - o, C)
+                remote(pick(send, frm), recv.at[frm], ss.at[o], rs.at[o], wide=2 * frm + core).wait_recv()
                 return c
-            lax.fori_loop(1, W, step, 0)
+            lax.fori_loop(1, C, step, 0)
 
         def left(send, recv, ss, rs, pick):
             def step(o, c):
-                to = lax.rem(me + o, W)
-                remote(pick(send, to), recv.at[me], ss.at[o], rs.at[o], wide=to).wait_send()
+                to = lax.rem(chip + o, C)
+                remote(pick(send, to), recv.at[chip], ss.at[o], rs.at[o], wide=2 * to + core).wait_send()
                 return c
-            lax.fori_loop(1, W, step, 0)
+            lax.fori_loop(1, C, step, 0)
 
         one = lambda ref, s: ref.at[s]
         two = lambda ref, s: ref.at[pl.ds(s, 2)]
@@ -272,25 +279,58 @@
             h = substitute(rs, [qy[y, rows(s), :] for y in range(Y - 1)], [iy[y, rows(s), :] for y in range(Y)])
             for y in range(Y):
                 hy[y, rows(s), :] = h[y]
-            rsend[s, 0] = h[0]
-            rsend[s, 1] = h[Y - 1]
+            xs[0, rows(s), :] = h[0]
+            xs[1, rows(s), :] = h[Y - 1]
         loop(W, y_rhs, 4)
         pl.semaphore_wait(barrier, W - 1 + N - 1)
+        side, far = pl.multiple_of(core * H, H), pl.multiple_of((1 - core) * H, H)
+        to_mate = remote(xs.at[:, pl.ds(far, H), :], xr, xs_s.at[0], xs_r.at[0], wide=mate)
+        to_mate.start()
+        skip = remote(cy.at[Y - 1, pl.ds(H, H), :], ccr, cc_s.at[0], cc_r.at[0], wide=lax.rem(me + 2, W))
+        skip_sends = jnp.logical_and(core == 1, me < W - 2)
+        skip_comes = jnp.logical_and(core == 1, me > 2)
+
+        @pl.when(skip_sends)
+        def _():
+            skip.start()
         start_pair(c_up, c_down)
-        exchange(rsend, rrecv, rs_s, rs_r, one)
-        rrecv[me] = rsend[me]
 
         recv_pair(c_up, c_down)
 
-        def fill(s):
-            w = HH * (chr_[0, rows(s), :] + cy[0, rows(s), :])
-            msend[s, 0] = v1y[0, rows(s), :] + 1.0 / w
-            msend[s, 1] = v8y[Y - 1, rows(s), :]
-            msend[s, 2] = v8y[0, rows(s), :]
-        loop(W, fill, 4)
-
+        @pl.when(core == 0)
+        def _():
+            ccr[...] = chr_[0, pl.ds(0, H), :]
+
+        @pl.when(skip_comes)
+        def _():
+            skip.wait_recv()
+
+        @pl.when(me == 1)
+        def _():
+            ccr[...] = jnp.zeros((H, Z), F32)
+        to_mate.wait_recv()
+        is_low = core == 0
+
+        def merge(g):
+            at = pl.ds(g * R, R)
+            own = [xs[i, pl.ds(side + g * R, R), :] for i in range(7)]
+            oth = [xr[i, at, :] for i in range(7)]
+            h1, h8, g1, gx, g8, c1, c8 = [jnp.where(is_low, a, b) for a, b in zip(own, oth)]
+            k1, k8, j1, jx, j8, d1, d8 = [jnp.where(is_low, b, a) for a, b in zip(own, oth)]
+            m = 1.0 / (1.0 / (HH * (c8 + d1)) + g8 + j1)
+            f = m * (h8 - k1)
+            alpha, beta = m * gx, m * jx
+            bf[at, :] = f
+            ba[at, :] = alpha
+            bb[at, :] = beta
+            msend[g, 0] = h1 - gx * f
+            msend[g, 1] = k8 + jx * f
+            msend[g, 2] = g1 - gx * alpha + 1.0 / (HH * (ccr[at, :] + c1))
+            msend[g, 3] = j8 - jx * beta
+            msend[g, 4] = jx * alpha
+        loop(C, merge, 4)
         exchange(msend, mrecv, ms_s, ms_r, one)
-        mrecv[me] = msend[me]
+        mrecv[chip] = msend[chip]
 
         loads[2].wait()
         for y in range(Y):
@@ -355,14 +395,6 @@
                 z_copy(buf, ss, rs, o, lax.rem(mine + o, N), mine).wait_send()
         z_send(zmat, zm_s, zm_r)
 
-        arrived(msend, mrecv, ms_s, ms_r, one)
-        m, k = chain_factor(
-            [mrecv[p, 0] + mrecv[p - 1, 1] for p in range(1, W)], [mrecv[p, 2] for p in range(1, W - 1)])
-        for p in range(W - 1):
-            sm[p] = m[p]
-            if p < W - 2:
-                sk[p] = k[p]
-
         z_recv(zmat, zm_s, zm_r)
         below, above = jnp.maximum(mine - 1, 0), jnp.minimum(mine + 1, N - 1)
         has_lo = jnp.where(mine > 0, 1.0, 0.0).astype(F32)
@@ -378,24 +410,45 @@
         for y in range(Y):
             lz[y] = rz[pl.ds(y, Z, stride=Y), :].T
 
-        arrived(rsend, rrecv, rs_s, rs_r, one)
-        f = chain_solve(
-            [rrecv[p - 1, 1] - rrecv[p, 0] for p in range(1, W)],
-            [sm[p] for p in range(W - 1)], [sk[p] for p in range(W - 2)])
+        arrived(msend, mrecv, ms_s, ms_r, one)
+        m, k = chain_factor(
+            [mrecv[p, 2] + mrecv[p - 1, 3] for p in range(1, C)], [mrecv[p, 4] for p in range(1, C - 1)])
+        f = chain_solve([mrecv[p - 1, 1] - mrecv[p, 0] for p in range(1, C)], m, k)
         edge = jnp.zeros((R, Z), F32)
         fs[0] = edge
-        fs[W] = edge
-        for p in range(1, W):
+        fs[C] = edge
+        for p in range(1, C):
             fs[p] = f[p - 1]
         exchange(fs, frecv, fs_s, fs_r, two)
-        frecv[me] = fs[pl.ds(me, 2)]
+        frecv[chip] = fs[pl.ds(chip, 2)]
         arrived(fs, frecv, fs_s, fs_r, two)
 
-        def y_final(s):
-            fl, fr = frecv[s, 0], frecv[s, 1]
+        def finish(at, fl, fr):
             for y in range(Y):
-                sec[y, rows(s), :] = hy[y, rows(s), :] + v1y[y, rows(s), :] * fl - v8y[y, rows(s), :] * fr
-        loop(W, y_final, 4)
+                sec[y, at, :] = hy[y, at, :] + v1y[y, at, :] * fl - v8y[y, at, :] * fr
+
+        def middle(g):
+            at = pl.ds(g * R, R)
+            fl, fr = frecv[g, 0], frecv[g, 1]
+            f = bf[at, :] + ba[at, :] * fl + bb[at, :] * fr
+            ps[0, at, :] = jnp.where(is_low, f, fl)
+            ps[1, at, :] = jnp.where(is_low, fr, f)
+        loop(C, middle, 4)
+        flux_mate = remote(ps, pr, ps_s.at[0], ps_r.at[0], wide=mate)
+        flux_mate.start()
+
+        def own_final(g):
+            fl, fr = frecv[g, 0], frecv[g, 1]
+            at = pl.ds(g * R, R)
+            f = jnp.where(is_low, ps[0, at, :], ps[1, at, :])
+            finish(pl.ds(side + g * R, R), jnp.where(is_low, fl, f), jnp.where(is_low, f, fr))
+        loop(C, own_final, 4)
+        flux_mate.wait_recv()
+
+        def mate_final(g):
+            at = pl.ds(g * R, R)
+            finish(pl.ds(far + g * R, R), pr[0, at, :], pr[1, at, :])
+        loop(C, mate_final, 4)
         for y in range(Y):
             rz[pl.ds(y, Z, stride=Y), :] = sec[y].T
 
@@ -482,7 +535,12 @@
         sent_pair(c_up, c_down)
         sent_pair(a_up, a_down)
         left(msend, mrecv, ms_s, ms_r, one)
-        left(rsend, rrecv, rs_s, rs_r, one)
+        to_mate.wait_send()
+        flux_mate.wait_send()
+
+        @pl.when(skip_sends)
+        def _():
+            skip.wait_send()
         left(fs, frecv, fs_s, fs_r, two)
         z_left(zmat, zm_s, zm_r)
         z_left(zrhs, zr_s, zr_r)
@@ -491,15 +549,17 @@
     planes = pltpu.VMEM((Y, X, Z), F32)
     flux = lambda count: pltpu.VMEM((count, Y, Z), F32)
     part = lambda *lead: pltpu.VMEM((*lead, R, Z), F32)
+    half = lambda *lead: pltpu.VMEM((*lead, H, Z), F32)
     sems = lambda count: pltpu.SemaphoreType.DMA((count,))
     scratch = [flat, flat, flat, flat, flat, flat, flat, flux(XB + 1), flat,
                planes, planes, planes, planes, planes, planes, planes,
-               part(W, 3), part(W, 3), part(W, 2), part(W, 2), part(W), part(W), part(W + 1), part(W, 2),
+               pltpu.VMEM((7, X, Z), F32), pltpu.VMEM((7, H, Z), F32), half(), half(), half(),
+               part(C, 5), part(C, 5), part(C), part(C), part(C + 1), part(C, 2), half(2), half(2),
                flat, flat, flat, flat, flat, flat, flat, flat,
                flux(ZB + 1), flux(ZB + 1), flux(ZB + 1), flux(ZB), flux(ZB),
                pltpu.VMEM((N, 7, Y, Z), F32), pltpu.VMEM((N, 2, Y, Z), F32), flux(N + 1), planes, planes,
-               pltpu.VMEM((8, Z), F32), pltpu.VMEM((2, X, Z), F32), pltpu.VMEM((2, X, Z), F32),
-               sems(W), sems(W), sems(W), sems(W), sems(W), sems(W), sems(N), sems(N), sems(N), sems(N),
+               half(), pltpu.VMEM((2, X, Z), F32), pltpu.VMEM((2, X, Z), F32),
+               sems(C), sems(C), sems(C), sems(C), sems(1), sems(1), sems(1), sems(1), sems(1), sems(1), sems(N), sems(N), sems(N), sems(N),
                sems(2), sems(2), sems(2), sems(2), sems(4)]
     return kernel, scratch
 
@@ -515,7 +575,7 @@
         results = pl.pallas_call(
             kernel,
             out_shape=(out, out),
-            in_specs=[pl.BlockSpec(memory_space=pl.ANY)] * 4,
+            in_specs=[pl.BlockSpec(memory_space=pltpu.HBM)] * 4,
             out_specs=(vmem, vmem),
             scratch_shapes=scratch,
             compiler_params=pltpu.CompilerParams(

time: 33.6 us -> 31.3 us (0.932)
  Pallas kernels: 30 us -> 27.8 us
    pallas_call x1, Pallas kernels: 30 us -> 27.8 us  [per_device(): pl.pallas_call(kernel, out_shape=(out, out), in_specs=[pl.BlockSpec(memor...]
where the time goes in v3:
time: 31.3 us; the launch traced here: 31.2 us
  Pallas kernels  27.8 us (89%)
  local copies, waits for them, and re-layouts  2.72 us (9%)
  between operations  0.65 us (2%)
    pallas_call x1, Pallas kernels, per_device(): pl.pallas_call(kernel, out_shape=(out, out), in_specs=[pl.BlockSpec(memor...  27.8 us
    unnamed x4, local copies, waits for them, and re-layouts  2.72 us

profile of v3, /device:TPU:1, one launch (start us, length us, event | category | flops | bytes accessed | tf_op | source)
XLA Modules:
  0.0 31.2 jit_solution(9991422394496285560)
XLA Ops:
  0.6 27.8 %shard_map.59 = (f32[1024,128]{1,0:T(8,128)}, f32[1024,128]{1,0:T(8,128)}) custom-call(f32[1024,128]{1,0:T(8,128)} %bitcast.8, f32[1024,128]{1,0:T(8,128)} %bitcast.9, f32[1024,128]{1,0:T(8,128)} %bitcast.10, f32[1024,128]{1,0:T(8,128)} %bitcast.11), custom_call_target="tpu_custom_call" | custom-call | tf_op jit(solution)/shard_map/pallas_call | solution.py:575
  28.4 0.0 copy-start
  28.4 1.9 %copy.8 = f32[128,8,128]{2,1,0:T(8,128)} copy(f32[128,8,128]{2,1,0:T(8,128)} %bitcast.7) | data formatting | bytes 1048576
  30.4 0.0 copy-done
  30.4 0.8 %copy.9 = f32[128,8,128]{2,1,0:T(8,128)} copy(f32[128,8,128]{2,1,0:T(8,128)S(1)} %bitcast.6) | data formatting | bytes 1048576
Async XLA Ops:
  28.4 1.9 %copy-start = (f32[1024,128]{1,0:T(8,128)S(1)}, f32[1024,128]{1,0:T(8,128)}, u32[]{:S(2)}) copy-start(f32[1024,128]{1,0:T(8,128)} %get-tuple-element.5) | copy-start | bytes 1572868

commit v4 on v3

--- a/solution.py
+++ b/solution.py
@@ -571,7 +571,7 @@
         X, Y, Z = arrays[0].shape
         kernel, scratch = make_kernel(W, N, X, Y, Z)
         vmem = pl.BlockSpec(memory_space=pltpu.VMEM)
-        out = jax.ShapeDtypeStruct((X * Y, Z), F32)
+        out = pltpu.VMEM((X * Y, Z), F32)
         results = pl.pallas_call(
             kernel,
             out_shape=(out, out),
@@ -579,7 +579,7 @@
             out_specs=(vmem, vmem),
             scratch_shapes=scratch,
             compiler_params=pltpu.CompilerParams(
-                collective_id=0, has_side_effects=True, vmem_limit_bytes=56 * 1024 * 1024),
+                collective_id=0, has_side_effects=True, vmem_limit_bytes=54 * 1024 * 1024),
         )(*[a.reshape(X * Y, Z) for a in arrays])
         return tuple(r.reshape(X, Y, Z) for r in results)
 

time: 31.3 us -> 29.2 us (0.933)
  local copies, waits for them, and re-layouts: 2.72 us -> 1.59 us
  Pallas kernels: 27.8 us -> 26.8 us
    unnamed x4 -> x2, local copies, waits for them, and re-layouts: 2.72 us -> 1.59 us
    pallas_call x1, Pallas kernels: 27.8 us -> 26.8 us  [per_device(): pl.pallas_call(kernel, out_shape=(out, out), in_specs=[pl.BlockSpec(memor...]
where the time goes in v4:
time: 29.2 us; the launch traced here: 29 us
  Pallas kernels  26.8 us (92%)
  local copies, waits for them, and re-layouts  1.59 us (5%)
  between operations  0.64 us (2%)
    pallas_call x1, Pallas kernels, per_device(): pl.pallas_call(kernel, out_shape=(out, out), in_specs=[pl.BlockSpec(memor...  26.8 us
    unnamed x2, local copies, waits for them, and re-layouts  1.59 us

profile of v4, /device:TPU:1, one launch (start us, length us, event | category | flops | bytes accessed | tf_op | source)
XLA Modules:
  0.0 29.0 jit_solution(14153862991360410016)
XLA Ops:
  0.6 26.8 %shard_map.59 = (f32[1024,128]{1,0:T(8,128)S(1)}, f32[1024,128]{1,0:T(8,128)S(1)}) custom-call(f32[1024,128]{1,0:T(8,128)} %bitcast.8, f32[1024,128]{1,0:T(8,128)} %bitcast.9, f32[1024,128]{1,0:T(8,128)} %bitcast.10, f32[1024,128]{1,0:T(8,128)} %bitcast.11), custom_call_target="tpu_custom_call" | custom-call | tf_op jit(solution)/shard_map/pallas_call | solution.py:575
  27.5 0.8 %copy.8 = f32[128,8,128]{2,1,0:T(8,128)} copy(f32[128,8,128]{2,1,0:T(8,128)S(1)} %bitcast.7) | data formatting | bytes 1048576
  28.2 0.8 %copy.9 = f32[128,8,128]{2,1,0:T(8,128)} copy(f32[128,8,128]{2,1,0:T(8,128)S(1)} %bitcast.6) | data formatting | bytes 1048576
